TPU v7x, 256 devices: a whole 4x4x8 slice. The times are simulated.
256 devices in a mesh: rowblk: 16 (over z, x_lo), colblk: 16 (over x_hi, y, core).
Axes of the slice: x: 4 (x_hi: 2, x_lo: 2; x = x_hi * 2 + x_lo), y: 4, z: 8, core: 2. Of those that a mesh axis runs over, the one named last changes fastest.
Arguments:
- points: bfloat16 [65536, 128], P(('rowblk', 'colblk')), may hold values from -6 to 6
- spread: float32 [1], replicated, may hold values from 2.5 to 3.5
- panel: bfloat16 [65536, 32], P(('rowblk', 'colblk')), may hold values from -6 to 6
Outputs:
- refined: float32 [32, 65536], P(None, ('rowblk', 'colblk'))
All inputs are finite; a program needn't handle non-finite values.
Results may differ from a plain program's by a relative error of at most 0.0055.
Values may be sent and summed in bfloat16 or wider, within the bound.
A program may use at most 64 MiB of HBM per device.

v0:
```python
import math

import jax
import jax.numpy as jnp
from jax import lax
from jax.sharding import PartitionSpec as P


def tile_terms(row_pts, row_ids, col_stack, col_ids, coef, width):
    col_pts = col_stack[:, :width]
    col_vals = col_stack[:, width:]
    col_sq = jnp.sum(jnp.square(col_pts.astype(jnp.float32)), axis=1)
    count = row_pts.shape[0]
    block = math.gcd(count, 512)

    def one_block(start):
        rows = lax.dynamic_slice_in_dim(row_pts, start, block, 0)
        ids = lax.dynamic_slice_in_dim(row_ids, start, block, 0)
        rows_sq = jnp.sum(jnp.square(rows.astype(jnp.float32)), axis=1)
        inner = lax.dot_general(
            rows, col_pts, (((1,), (1,)), ((), ())), preferred_element_type=jnp.float32
        )
        expo = (rows_sq[:, None] + col_sq[None, :] - 2.0 * inner) * coef
        affinity = jnp.where(
            ids[:, None] != col_ids[None, :], jnp.exp(expo), jnp.float32(0.0)
        ).astype(jnp.bfloat16)
        degree = jnp.sum(affinity.astype(jnp.float32), axis=1)
        product = jnp.dot(affinity, col_vals, preferred_element_type=jnp.float32)
        return (product, degree)

    starts = jnp.arange(count // block, dtype=jnp.int32) * block
    product, degree = lax.map(one_block, starts)
    return (product.reshape(count, col_vals.shape[1]), degree.reshape(count))


def per_device(points, spread, panel):
    n_col = lax.axis_size("colblk")
    n_row = lax.axis_size("rowblk")
    row_index = lax.axis_index("rowblk")
    col_index = lax.axis_index("colblk")
    local = points.shape[0]
    width = points.shape[1]
    total = local * n_row * n_col
    coef = -0.5 / (spread[0] * spread[0])
    stacked = jnp.concatenate([points, panel], axis=1)
    rows_base = row_index * (n_col * local)
    row_pts = lax.all_gather(points, "colblk", axis=0, tiled=True)
    row_ids = rows_base + jnp.arange(row_pts.shape[0], dtype=jnp.int32)
    piece = (lax.all_gather(stacked, "rowblk", axis=0, tiled=True),)[0]
    place = jnp.arange(piece.shape[0], dtype=jnp.int32)
    product, degree = tile_terms(
        row_pts,
        row_ids,
        piece,
        (place // local * n_col + col_index) * local + place % local,
        coef,
        width,
    )
    product, degree = (product, degree)
    product_own, degree_own = (
        lax.psum_scatter(product, "colblk", scatter_dimension=0, tiled=True),
        lax.psum_scatter(degree, "colblk", scatter_dimension=0, tiled=True),
    )
    walked = product_own / degree_own[:, None]
    sums = lax.psum(jnp.sum(walked * walked, axis=0), ("rowblk", "colblk"))
    scale = jnp.sqrt(sums / total + 1e-06)
    return (walked / scale[None, :]).T


def solution(mesh):
    return jax.shard_map(
        per_device,
        mesh=mesh,
        in_specs=(P(("rowblk", "colblk"), None), P(), P(("rowblk", "colblk"), None)),
        out_specs=P(None, ("rowblk", "colblk")),
        check_vma=False,
    )
```

profile of v0, /device:TPU:1, one launch (start us, length us, event | category | flops | bytes accessed | tf_op | source)
XLA Modules:
  0.0 370.9 jit_solution(9305807805707385960)
XLA Ops:
  7.4 1.5 pad_maximum_fusion
  10.4 66.4 %all-gather.5.cloned.1.call-done = bf16[4096,160]{1,0:T(8,128)(2,1)} async-done(((bf16[256,160]{1,0:T(8,128)(2,1)}), bf16[4096,160]{1,0:T(8,128)(2,1)}) %all-gather.5.cloned.1.call-update) | async-done | bytes 1310736 | tf_op jit(solution)/shard_map/all_gather | solution.py:49
  76.8 1.4 slice.8
  80.2 56.9 %all-gather.3.cloned.1.call-done = bf16[4096,128]{1,0:T(8,128)(2,1)} async-done(((bf16[256,128]{1,0:T(8,128)(2,1)}), bf16[4096,128]{1,0:T(8,128)(2,1)}) %all-gather.3.cloned.1.call-update) | async-done | bytes 1048592 | tf_op jit(solution)/shard_map/all_gather | solution.py:47
  137.1 76.7 %while.13 = (s32[]{:T(128)}, f32[8,512,32]{1,0,2:T(8,128)S(1)}, f32[8,512]{1,0:T(8,128)S(1)}, s32[8]{0:T(128)S(1)}, s32[4096]{0:T(1024)S(1)}, /*index=5*/bf16[40...) while((s32[]{:T(128)}, f32[8,512,32]{1,0,2:T(8,128)S(1)}, ...), condition=%wide.region_4.5_spmd.clone, body=%wide.region_1.4_spmd.clone.sunk | while | flops 690224128 | bytes 10355403 | solution.py:32
  140.5 4.1 %convert_reduce_fusion.2 = (f32[512]{0:T(512)S(1)}, bf16[512,4096]{1,0:T(8,128)(2,1)S(1)}) fusion(f32[]{:T(128)} %get-tuple-element.221, bf16[4096,128]{1,0:T(8,128)(2,1)S(1)} %get-tuple-element.220, bf16[4096,128]{1,0:T(8,128)(2,1)} %get-tuple-element.218, s32[]{:T(128)S(6)} %select_n.50, f32[4096]{0:T(1024)S(1)} %get-tuple-element.219, ...), kind=kOutput, calls=%fused_computation.1.clone.1 | convolution fusion | flops 555744768 | bytes 5413380 | tf_op jit(solution)/shard_map/while/body/eval_jaxpr/dot_general | solution.py:20
  144.6 1.3 convolution_bitcast_fusion.2
  150.0 4.1 %convert_reduce_fusion.2 = (f32[512]{0:T(512)S(1)}, bf16[512,4096]{1,0:T(8,128)(2,1)S(1)}) fusion(f32[]{:T(128)} %get-tuple-element.221, bf16[4096,128]{1,0:T(8,128)(2,1)S(1)} %get-tuple-element.220, bf16[4096,128]{1,0:T(8,128)(2,1)} %get-tuple-element.218, s32[]{:T(128)S(6)} %select_n.50, f32[4096]{0:T(1024)S(1)} %get-tuple-element.219, ...), kind=kOutput, calls=%fused_computation.1.clone.1 | convolution fusion | flops 555744768 | bytes 5413380 | tf_op jit(solution)/shard_map/while/body/eval_jaxpr/dot_general | solution.py:20
  154.2 1.3 convolution_bitcast_fusion.2
  159.6 4.1 %convert_reduce_fusion.2 = (f32[512]{0:T(512)S(1)}, bf16[512,4096]{1,0:T(8,128)(2,1)S(1)}) fusion(f32[]{:T(128)} %get-tuple-element.221, bf16[4096,128]{1,0:T(8,128)(2,1)S(1)} %get-tuple-element.220, bf16[4096,128]{1,0:T(8,128)(2,1)} %get-tuple-element.218, s32[]{:T(128)S(6)} %select_n.50, f32[4096]{0:T(1024)S(1)} %get-tuple-element.219, ...), kind=kOutput, calls=%fused_computation.1.clone.1 | convolution fusion | flops 555744768 | bytes 5413380 | tf_op jit(solution)/shard_map/while/body/eval_jaxpr/dot_general | solution.py:20
  163.8 1.3 convolution_bitcast_fusion.2
  169.2 4.1 %convert_reduce_fusion.2 = (f32[512]{0:T(512)S(1)}, bf16[512,4096]{1,0:T(8,128)(2,1)S(1)}) fusion(f32[]{:T(128)} %get-tuple-element.221, bf16[4096,128]{1,0:T(8,128)(2,1)S(1)} %get-tuple-element.220, bf16[4096,128]{1,0:T(8,128)(2,1)} %get-tuple-element.218, s32[]{:T(128)S(6)} %select_n.50, f32[4096]{0:T(1024)S(1)} %get-tuple-element.219, ...), kind=kOutput, calls=%fused_computation.1.clone.1 | convolution fusion | flops 555744768 | bytes 5413380 | tf_op jit(solution)/shard_map/while/body/eval_jaxpr/dot_general | solution.py:20
  173.4 1.3 convolution_bitcast_fusion.2
  178.8 4.1 %convert_reduce_fusion.2 = (f32[512]{0:T(512)S(1)}, bf16[512,4096]{1,0:T(8,128)(2,1)S(1)}) fusion(f32[]{:T(128)} %get-tuple-element.221, bf16[4096,128]{1,0:T(8,128)(2,1)S(1)} %get-tuple-element.220, bf16[4096,128]{1,0:T(8,128)(2,1)} %get-tuple-element.218, s32[]{:T(128)S(6)} %select_n.50, f32[4096]{0:T(1024)S(1)} %get-tuple-element.219, ...), kind=kOutput, calls=%fused_computation.1.clone.1 | convolution fusion | flops 555744768 | bytes 5413380 | tf_op jit(solution)/shard_map/while/body/eval_jaxpr/dot_general | solution.py:20
  182.9 1.3 convolution_bitcast_fusion.2
  188.4 4.1 %convert_reduce_fusion.2 = (f32[512]{0:T(512)S(1)}, bf16[512,4096]{1,0:T(8,128)(2,1)S(1)}) fusion(f32[]{:T(128)} %get-tuple-element.221, bf16[4096,128]{1,0:T(8,128)(2,1)S(1)} %get-tuple-element.220, bf16[4096,128]{1,0:T(8,128)(2,1)} %get-tuple-element.218, s32[]{:T(128)S(6)} %select_n.50, f32[4096]{0:T(1024)S(1)} %get-tuple-element.219, ...), kind=kOutput, calls=%fused_computation.1.clone.1 | convolution fusion | flops 555744768 | bytes 5413380 | tf_op jit(solution)/shard_map/while/body/eval_jaxpr/dot_general | solution.py:20
  192.5 1.3 convolution_bitcast_fusion.2
  198.0 4.1 %convert_reduce_fusion.2 = (f32[512]{0:T(512)S(1)}, bf16[512,4096]{1,0:T(8,128)(2,1)S(1)}) fusion(f32[]{:T(128)} %get-tuple-element.221, bf16[4096,128]{1,0:T(8,128)(2,1)S(1)} %get-tuple-element.220, bf16[4096,128]{1,0:T(8,128)(2,1)} %get-tuple-element.218, s32[]{:T(128)S(6)} %select_n.50, f32[4096]{0:T(1024)S(1)} %get-tuple-element.219, ...), kind=kOutput, calls=%fused_computation.1.clone.1 | convolution fusion | flops 555744768 | bytes 5413380 | tf_op jit(solution)/shard_map/while/body/eval_jaxpr/dot_general | solution.py:20
  202.1 1.3 convolution_bitcast_fusion.2
  207.6 4.1 %convert_reduce_fusion.2 = (f32[512]{0:T(512)S(1)}, bf16[512,4096]{1,0:T(8,128)(2,1)S(1)}) fusion(f32[]{:T(128)} %get-tuple-element.221, bf16[4096,128]{1,0:T(8,128)(2,1)S(1)} %get-tuple-element.220, bf16[4096,128]{1,0:T(8,128)(2,1)} %get-tuple-element.218, s32[]{:T(128)S(6)} %select_n.50, f32[4096]{0:T(1024)S(1)} %get-tuple-element.219, ...), kind=kOutput, calls=%fused_computation.1.clone.1 | convolution fusion | flops 555744768 | bytes 5413380 | tf_op jit(solution)/shard_map/while/body/eval_jaxpr/dot_general | solution.py:20
  216.2 61.3 %all-reduce = f32[4096]{0:T(1024)S(1)} all-reduce(f32[4096]{0:T(1024)S(1)} %bitcast.31), channel_id=3, replica_groups=mesh['rowblk'=16,'colblk'=16] {'colblk'}, use_global_device_ids=true, to_apply=%region_6.7.clone | all-reduce | flops 4096 | bytes 32768
  277.5 7.1 %reduce-scatter.2.cloned.1.call-done = f32[256,32]{0,1:T(8,128)} async-done(((f32[4096,32]{0,1:T(8,128)}), f32[256,32]{0,1:T(8,128)}) %reduce-scatter.2.cloned.1.call-update) | async-done | bytes 32784 | tf_op jit(solution)/shard_map/reduce_scatter | solution.py:61
  285.5 77.4 %psum.7 = f32[32]{0:T(128)S(1)} all-reduce(f32[32]{0:T(128)S(1)} %multiply_reduce_fusion.2), channel_id=1, replica_groups=mesh['rowblk'=16,'colblk'=16] {'rowblk','colblk'}, use_global_device_ids=true, to_apply=%region_8.9 | all-reduce | flops 32 | bytes 256 | tf_op jit(solution)/shard_map/psum | solution.py:65
  362.9 1.5 divide_bitcast_fusion
  (80 shorter events, 27.0 us)
Async XLA Ops:
  6.5 70.3 %all-gather.5.cloned.1.call-start = ((), (), s32[]{:S(2)}) async-start(), calls=%async_computation.2 | async-start | bytes 2228224 | tf_op jit(solution)/shard_map/all_gather | solution.py:49
  8.9 128.2 %all-gather.3.cloned.1.call-start = ((), (), s32[]{:S(2)}) async-start(), calls=%async_computation.1 | async-start | bytes 1114112 | tf_op jit(solution)/shard_map/all_gather | solution.py:47
  9.7 275.0 %reduce-scatter.2.cloned.1.call-start = ((), (), s32[]{:S(2)}) async-start(), calls=%async_computation.3 | async-start | bytes 557056 | tf_op jit(solution)/shard_map/reduce_scatter | solution.py:61
  76.8 2.7 copy-start
  137.1 77.8 %copy-start.1 = (u32[256]{0:T(256)S(1)}, u32[256]{0:T(256)}, u32[]{:S(2)}) copy-start(u32[256]{0:T(256)} %constant.76) | copy-start | bytes 3076
Sparse Core Ops, SparseCore 0:
  9.1 67.6 all-gather.4
  79.6 57.4 all-gather.2
  215.0 69.5 reduce-scatter.1
where the time goes:
time: 372 us; the launch traced here: 371 us
  blocking collectives  139 us (37%)
  waiting for transfers between devices  131 us (35%)
  matrix products  43.6 us (12%)
  local copies, waits for them, and re-layouts  16.3 us (4%)
  between operations  14.5 us (4%)
  loops' own time  13.5 us (4%)
  other arithmetic  13 us (3%)
    psum x1, blocking collectives, per_device(): sums = lax.psum(jnp.sum(walked * walked, axis=0), ('rowblk', 'colblk'))  77.4 us
    all_gather x1, waiting for transfers between devices, per_device(): piece = (lax.all_gather(stacked, 'rowblk', axis=0, tiled=True),)[0]  66.4 us
    unnamed x1, blocking collectives  61.3 us
    all_gather x1, waiting for transfers between devices, per_device(): row_pts = lax.all_gather(points, 'colblk', axis=0, tiled=True)  56.9 us
    dot_general x8, matrix products, one_block(): lax.dot_general(rows, col_pts, (((1,), (1,)), ((), ())), preferred_elemen...  33.1 us
    another operation x1, loops' own time, tile_terms(): product, degree = lax.map(one_block, starts)  13.5 us
    dot_general x8, matrix products, one_block(): product = jnp.dot(affinity, col_vals, preferred_element_type=jnp.float32)  10.6 us
    reduce_sum x8, other arithmetic, one_block(): rows_sq = jnp.sum(jnp.square(rows.astype(jnp.float32)), axis=1)  8.43 us
  transfers between devices with their start and end apart: 3, of which 3 were waited for; matrix products, arithmetic and copies ran while one was open for 1% of the time, Pallas kernels for 0%

commit v1 on v0

v1 whole, which is shorter than its diff:
```python
import functools
import math

import jax
import jax.numpy as jnp
from jax import lax
from jax.experimental import pallas as pl
from jax.experimental.pallas import tpu as pltpu

MESH = pl.DeviceIdType.MESH
LOG2E = math.log2(math.e)
B = 256
W = 128
KC = 32
KR = 48
AUG = 16
NX, NY, NZ = 4, 4, 8


def three_terms(v):
    hi = v.astype(jnp.bfloat16)
    rest = v - hi.astype(jnp.float32)
    mid = rest.astype(jnp.bfloat16)
    lo = (rest - mid.astype(jnp.float32)).astype(jnp.bfloat16)
    return hi, mid, lo


def kernel(
    total,
    spread_ref, points_ref, panel_ref, out_ref,
    rows, cols, colaug, pt, acc, sendp, recvp, st_send, st_recv,
    row_s, row_r, col_s, col_r, colp_s, colp_r, red_s, red_r, a_s, a_r, b_s, b_r,
):
    r = lax.axis_index("rowblk")
    c = lax.axis_index("colblk")
    z, xl = r // 2, r % 2
    xh, y, core = c // 8, (c // 2) % 4, c % 2
    x = xh * 2 + xl

    def dev(xx, yy, zz, cc):
        return {"rowblk": zz * 2 + xx % 2, "colblk": ((xx // 2) * 4 + yy) * 2 + cc}

    def plane(s):
        dx, dy = s // 4, s % 4
        return dev((x + dx) % 4, (y + dy) % 4, z, core)

    def plane_back(s):
        dx, dy = s // 4, s % 4
        return ((4 - dx) % 4) * 4 + (4 - dy) % 4

    def line(s):
        dz, dc = s // 2, s % 2
        return dev(x, y, (z + dz) % 8, (core + dc) % 2)

    def line_back(s):
        dz, dc = s // 2, s % 2
        return ((8 - dz) % 8) * 2 + dc

    barrier = pltpu.get_barrier_semaphore()
    for s in range(1, 16):
        pl.semaphore_signal(barrier, inc=1, device_id=plane(s), device_id_type=MESH)
        pl.semaphore_signal(barrier, inc=1, device_id=line(s), device_id_type=MESH)

    pts = points_ref[...]
    ptsf = pts.astype(jnp.float32)
    ptst = ptsf.T
    sq = -0.5 * jnp.sum(ptst * ptst, axis=0, keepdims=True)
    hi, mid, lo = three_terms(sq)
    row = lax.broadcasted_iota(jnp.int32, (AUG, B), 0)
    f = lambda t: t.astype(jnp.float32)
    aug = jnp.where(row == 0, f(hi), jnp.where(row == 1, f(mid), jnp.where(row == 2, f(lo), 0.0)))
    aug = jnp.where((row >= 3) & (row < 6), 1.0, aug)
    rows[0, :W, :] = ptst.astype(jnp.bfloat16)
    rows[0, W:W + AUG, :] = aug.astype(jnp.bfloat16)
    cols[0] = pts
    pt[0, :KC, :] = panel_ref[...]

    pl.semaphore_wait(barrier, 30)

    row_copies, col_copies = [], []
    for s in range(1, 16):
        cp = pltpu.make_async_remote_copy(
            src_ref=rows.at[0, pl.ds(0, W + AUG)], dst_ref=rows.at[plane_back(s), pl.ds(0, W + AUG)],
            send_sem=row_s.at[s], recv_sem=row_r.at[plane_back(s)],
            device_id=plane(s), device_id_type=MESH)
        cp.start()
        row_copies.append(cp)
        cp = pltpu.make_async_remote_copy(
            src_ref=cols.at[0], dst_ref=cols.at[line_back(s)],
            send_sem=col_s.at[s], recv_sem=col_r.at[line_back(s)],
            device_id=line(s), device_id_type=MESH)
        cp.start()
        cp2 = pltpu.make_async_remote_copy(
            src_ref=pt.at[0, pl.ds(0, KC)], dst_ref=pt.at[line_back(s), pl.ds(0, KC)],
            send_sem=colp_s.at[s], recv_sem=colp_r.at[line_back(s)],
            device_id=line(s), device_id_type=MESH)
        cp2.start()
        col_copies.append((cp, cp2))

    tail = jnp.where(lax.broadcasted_iota(jnp.int32, (KR - KC, B), 0) == 0, 1.0, 0.0).astype(jnp.bfloat16)

    def fill(s, _):
        rows[s, W + AUG:, :] = jnp.zeros((W - AUG, B), jnp.bfloat16)
        pt[s, KC:, :] = tail
        return 0
    lax.fori_loop(0, 16, fill, 0)
    acc[...] = jnp.zeros_like(acc)

    coef = LOG2E / (spread_ref[0] * spread_ref[0])

    def column_block(s, masked):
        xj = cols[s]
        xf = xj.astype(jnp.float32)
        sqj = -0.5 * jnp.sum(xf * xf, axis=1, keepdims=True)
        jh, jm, jl = three_terms(sqj)
        lane = lax.broadcasted_iota(jnp.int32, (B, W), 1)
        ja = jnp.where(lane < 3, 1.0, jnp.where(lane == 3, f(jh), jnp.where(lane == 4, f(jm), jnp.where(lane == 5, f(jl), 0.0))))
        lhs = jnp.concatenate([xj, ja.astype(jnp.bfloat16)], axis=1)
        for i in range(16):
            g = jnp.dot(lhs, rows[i], preferred_element_type=jnp.float32)
            a = jnp.exp2(g * coef)
            if masked and i == 0:
                eye = lax.broadcasted_iota(jnp.int32, (B, B), 0) == lax.broadcasted_iota(jnp.int32, (B, B), 1)
                a = jnp.where(eye, 0.0, a)
            acc[i] += jnp.dot(pt[s], a.astype(jnp.bfloat16), preferred_element_type=jnp.float32)

    for cp in row_copies:
        cp.wait_recv()
    column_block(0, True)

    def step(s, _):
        pltpu.make_async_remote_copy(
            src_ref=cols.at[0], dst_ref=cols.at[s], send_sem=col_s.at[s], recv_sem=col_r.at[s],
            device_id=line(1), device_id_type=MESH).wait_recv()
        pltpu.make_async_remote_copy(
            src_ref=pt.at[0, pl.ds(0, KC)], dst_ref=pt.at[s, pl.ds(0, KC)], send_sem=colp_s.at[s], recv_sem=colp_r.at[s],
            device_id=line(1), device_id_type=MESH).wait_recv()
        column_block(s, False)
        return 0
    lax.fori_loop(1, 16, step, 0)

    red = []
    for s in range(1, 16):
        cp = pltpu.make_async_remote_copy(
            src_ref=acc.at[s, pl.ds(0, 40)], dst_ref=recvp.at[plane_back(s)],
            send_sem=red_s.at[s], recv_sem=red_r.at[plane_back(s)],
            device_id=plane(s), device_id_type=MESH)
        cp.start()
        red.append(cp)
    sums = acc[0, :40, :]
    for cp in red:
        cp.wait_recv()
    for s in range(1, 16):
        sums = sums + recvp[s]
    walked = sums[:KC, :] / sums[KC:KC + 1, :]

    part = jnp.sum(walked * walked, axis=1, keepdims=True)
    diag = lax.broadcasted_iota(jnp.int32, (KC, 128), 0) == lax.broadcasted_iota(jnp.int32, (KC, 128), 1)
    flat = jnp.sum(jnp.where(diag, part, 0.0), axis=0, keepdims=True)

    def stage(k, flat, where, back, ss, rs):
        st_send[k] = jnp.broadcast_to(flat, (8, 128))
        cps = []
        for s in range(1, 16):
            cp = pltpu.make_async_remote_copy(
                src_ref=st_send.at[k], dst_ref=st_recv.at[k, back(s)],
                send_sem=ss.at[s], recv_sem=rs.at[back(s)],
                device_id=where(s), device_id_type=MESH)
            cp.start()
            cps.append(cp)
        for cp in cps:
            cp.wait_recv()
        for s in range(1, 16):
            flat = flat + st_recv[k, s, 0:1, :]
        return flat, cps

    flat, c1 = stage(0, flat, plane, plane_back, a_s, a_r)
    flat, c2 = stage(1, flat, line, line_back, b_s, b_r)
    mean = jnp.sum(jnp.where(diag, jnp.broadcast_to(flat, (KC, 128)), 0.0), axis=1, keepdims=True) / total
    out_ref[...] = walked / jnp.sqrt(mean + 1e-6)

    for cp in row_copies + red + c1 + c2:
        cp.wait_send()
    for cp, cp2 in col_copies:
        cp.wait_send()
        cp2.wait_send()


def per_device(total, points, spread, panel):
    dma = pltpu.SemaphoreType.DMA((16,))
    return pl.pallas_call(
        functools.partial(kernel, total),
        out_shape=jax.ShapeDtypeStruct((KC, B), jnp.float32),
        in_specs=[pl.BlockSpec(memory_space=pltpu.SMEM)] + [pl.BlockSpec(memory_space=pltpu.VMEM)] * 2,
        out_specs=pl.BlockSpec(memory_space=pltpu.VMEM),
        scratch_shapes=[
            pltpu.VMEM((16, 2 * W, B), jnp.bfloat16),
            pltpu.VMEM((16, B, W), jnp.bfloat16),
            pltpu.VMEM((16, B, W), jnp.bfloat16),
            pltpu.VMEM((16, KR, B), jnp.bfloat16),
            pltpu.VMEM((16, KR, B), jnp.float32),
            pltpu.VMEM((16, 40, B), jnp.float32),
            pltpu.VMEM((16, 40, B), jnp.float32),
            pltpu.VMEM((2, 8, 128), jnp.float32),
            pltpu.VMEM((2, 16, 8, 128), jnp.float32),
        ] + [dma] * 12,
        compiler_params=pltpu.CompilerParams(
            collective_id=0, has_side_effects=True, vmem_limit_bytes=48 << 20),
        cost_estimate=pl.CostEstimate(flops=2 * 4096 * 4096 * 160, bytes_accessed=1 << 20, transcendentals=4096 * 4096),
        name="walk",
    )(spread, points, panel.T)


def solution(mesh):
    P = jax.sharding.PartitionSpec
    total = float(B * mesh.size)
    return jax.shard_map(
        functools.partial(per_device, total),
        mesh=mesh,
        in_specs=(P(("rowblk", "colblk"), None), P(), P(("rowblk", "colblk"), None)),
        out_specs=P(None, ("rowblk", "colblk")),
        check_vma=False,
    )
```

time: 372 us -> 117 us (0.31)
  blocking collectives: 139 us -> 0 us
  waiting for transfers between devices: 131 us -> 0 us
  Pallas kernels: 0 us -> 114 us
  matrix products: 43.6 us -> 0 us
  local copies, waits for them, and re-layouts: 16.3 us -> 2.17 us
  between operations: 14.5 us -> 0.67 us
  loops' own time: 13.5 us -> 0 us
  other arithmetic: 13 us -> 0 us
    all_gather x2 -> x0, waiting for transfers between devices: 123 us -> none  [the longest x1 66.4 us: per_device(): piece = (lax.all_gather(stacked, 'rowblk', axis=0, tiled=True),)[0]]
    pallas_call x0 -> x1, Pallas kernels: none -> 114 us  [per_device(): pl.pallas_call(functools.partial(kernel, total), out_shape=jax.ShapeDtype...]
    psum x1 -> x0, blocking collectives: 77.4 us -> none  [per_device(): sums = lax.psum(jnp.sum(walked * walked, axis=0), ('rowblk', 'colblk'))]
    unnamed x1 -> x0, blocking collectives: 61.3 us -> none
    dot_general x16 -> x0, matrix products: 43.6 us -> none  [the longest x8 33.1 us: one_block(): lax.dot_general(rows, col_pts, (((1,), (1,)), ((), ())), preferred_elemen...]
    another operation x1 -> x0, loops' own time: 13.5 us -> none  [tile_terms(): product, degree = lax.map(one_block, starts)]
    reduce_sum x10 -> x0, other arithmetic: 9.92 us -> none  [the longest x8 8.43 us: one_block(): rows_sq = jnp.sum(jnp.square(rows.astype(jnp.float32)), axis=1)]
    reduce_scatter x1 -> x0, waiting for transfers between devices: 7.12 us -> none  [per_device(): lax.psum_scatter(product, 'colblk', scatter_dimension=0, tiled=True)]
  transfers between devices with their start and end apart: 3 -> 0, of which waited for: 3 -> 0; matrix products, arithmetic and copies ran while one was open for 1% -> 0% of each run, Pallas kernels for 0% -> 0%
where the time goes in v1:
time: 117 us
  Pallas kernels  114 us (97%)
  local copies, waits for them, and re-layouts  2.17 us (2%)
    pallas_call x1, Pallas kernels, per_device(): pl.pallas_call(functools.partial(kernel, total), out_shape=jax.ShapeDtype...  114 us

profile of v1, /device:TPU:1, one launch (start us, length us, event | category | flops | bytes accessed | tf_op | source)
XLA Modules:
  0.0 116.6 jit_solution(11154563727008491738)
XLA Ops:
  0.7 0.0 copy-start
  0.7 0.8 copy-done
  1.5 0.0 copy-start.1
  1.5 0.7 copy-done.1
  2.2 113.7 %walk.1 = f32[32,256]{1,0:T(8,128)S(1)} custom-call(f32[1]{0:T(128)S(6)} %copy.5.spread_ref, bf16[256,128]{1,0:T(8,128)(2,1)S(1)} %copy-done, bf16[32,256]{1,0:T(8,128)(2,1)S(1)} %bitcast.1), custom_call_target="tpu_custom_call" | custom-call | flops 5368709120 | bytes 1048576 | tf_op jit(solution)/shard_map/walk/pallas_call | solution.py:191
  115.9 0.6 copy.6
Async XLA Ops:
  0.7 0.8 copy-start
  1.5 0.7 copy-start.1

commit v2 on v1

v2 whole, which is shorter than its diff:
```python
import functools
import math

import jax
import jax.numpy as jnp
from jax import lax
from jax.experimental import pallas as pl
from jax.experimental.pallas import tpu as pltpu

MESH = pl.DeviceIdType.MESH
LOG2E = math.log2(math.e)
B = 256
W = 128
KC = 32
KR = 48
KS = 40
AUG = 16
G = 4
MSG = B + 2 * KC

PLANE = (
    (0, 0), (0, 1), (0, 3), (1, 0), (3, 0), (0, 2), (1, 1), (1, 3),
    (2, 0), (3, 1), (3, 3), (1, 2), (2, 1), (2, 3), (3, 2), (2, 2),
)
LINE = tuple((dz, dc) for dz in (0, 1, 7, 2, 6, 3, 5, 4) for dc in (0, 1))


def plane_back(s):
    dx, dy = PLANE[s]
    return PLANE.index(((4 - dx) % 4, (4 - dy) % 4))


def line_back(s):
    dz, dc = LINE[s]
    return LINE.index(((8 - dz) % 8, dc))


def three_terms(v):
    hi = v.astype(jnp.bfloat16).astype(jnp.float32)
    mid = (v - hi).astype(jnp.bfloat16).astype(jnp.float32)
    return hi, mid, v - hi - mid


def kernel(
    total,
    spread_ref, points_ref, panel_ref, out_ref,
    rows, cols, colaug, acc, recvp, st_send, st_recv,
    row_s, row_r, col_s, col_r, sib_s, fwd_s, red_s, red_r, a_s, a_r, b_s, b_r,
):
    r = lax.axis_index("rowblk")
    c = lax.axis_index("colblk")
    z, xl = r // 2, r % 2
    xh, y, core = c // 8, (c // 2) % 4, c % 2
    x = xh * 2 + xl

    def dev(xx, yy, zz, cc):
        return {"rowblk": zz * 2 + xx % 2, "colblk": ((xx // 2) * 4 + yy) * 2 + cc}

    def plane(s):
        dx, dy = PLANE[s]
        return dev((x + dx) % 4, (y + dy) % 4, z, core)

    def line(s):
        dz, dc = LINE[s]
        return dev(x, y, (z + dz) % 8, (core + dc) % 2)

    barrier = pltpu.get_barrier_semaphore()
    for s in range(1, 16):
        pl.semaphore_signal(barrier, inc=1, device_id=plane(s), device_id_type=MESH)
        pl.semaphore_signal(barrier, inc=1, device_id=line(s), device_id_type=MESH)

    pts = points_ref[...]
    ptst = pts.astype(jnp.float32).T
    hi, mid, lo = three_terms(-0.5 * jnp.sum(ptst * ptst, axis=0, keepdims=True))
    row = lax.broadcasted_iota(jnp.int32, (AUG, B), 0)
    aug = jnp.where(row == 0, hi, jnp.where(row == 1, mid, jnp.where(row == 2, lo, 0.0)))
    aug = jnp.where((row >= 3) & (row < 6), 1.0, aug)
    rows[0, :W, :] = ptst.astype(jnp.bfloat16)
    rows[0, W:W + AUG, :] = aug.astype(jnp.bfloat16)
    cols[0, :B, :] = pts
    cols[0, B:B + KC, :] = panel_ref[:, :W]
    cols[0, B + KC:, :] = panel_ref[:, W:]

    def fill(s, _):
        rows[s, W + AUG:, :] = jnp.zeros((W - AUG, B), jnp.bfloat16)
        return 0
    lax.fori_loop(0, 16, fill, 0)
    acc[...] = jnp.zeros_like(acc)

    coef = LOG2E / (spread_ref[0] * spread_ref[0])

    def augment(s):
        xf = cols[s, :B, :].astype(jnp.float32)
        jh, jm, jl = three_terms(-0.5 * jnp.sum(xf * xf, axis=1, keepdims=True))
        lane = lax.broadcasted_iota(jnp.int32, (B, W), 1)
        ja = jnp.where(lane == 3, jh, jnp.where(lane == 4, jm, jnp.where(lane == 5, jl, 0.0)))
        colaug[s] = jnp.where(lane < 3, 1.0, ja).astype(jnp.bfloat16)

    augment(0)

    pl.semaphore_wait(barrier, 30)

    def row_copy(s):
        t = plane_back(s)
        return pltpu.make_async_remote_copy(
            src_ref=rows.at[0, pl.ds(0, W + AUG)], dst_ref=rows.at[t, pl.ds(0, W + AUG)],
            send_sem=row_s.at[s], recv_sem=row_r.at[t], device_id=plane(s), device_id_type=MESH)

    def col_copy(src, dst, sem, where):
        return pltpu.make_async_remote_copy(
            src_ref=cols.at[src], dst_ref=cols.at[dst],
            send_sem=sem, recv_sem=col_r.at[dst], device_id=where, device_id_type=MESH)

    def sibling_copy(s):
        return col_copy(s, s + 1, sib_s.at[s // 2], line(1))

    def wait_col(s):
        col_copy(0, s, sib_s.at[0], line(1)).wait_recv()

    col_sends = [sibling_copy(0)]
    col_sends += [col_copy(0, line_back(s), col_s.at[s], line(s)) for s in (2, 4, 6, 8)]
    row_sends = [row_copy(s) for s in range(1, 16)]
    for cp in col_sends[:3] + row_sends[:3] + col_sends[3:] + row_sends[3:]:
        cp.start()

    pass_on = {
        6: col_copy(6, 10, fwd_s.at[0], line(4)),
        8: col_copy(8, 12, fwd_s.at[1], line(2)),
        10: col_copy(10, 14, fwd_s.at[2], line(4)),
    }
    siblings = {s: sibling_copy(s) for s in range(2, 16, 2)}

    wait_col(2)
    siblings[2].start()
    wait_col(1)
    augment(1)
    augment(2)
    wait_col(3)
    augment(3)

    def reduce_copy(s):
        t = plane_back(s)
        return pltpu.make_async_remote_copy(
            src_ref=acc.at[s, pl.ds(0, KS)], dst_ref=recvp.at[t],
            send_sem=red_s.at[s], recv_sem=red_r.at[t], device_id=plane(s), device_id_type=MESH)

    red = {s: reduce_copy(s) for s in range(1, 16)}
    ones = jnp.where(lax.broadcasted_iota(jnp.int32, (KR - KC, G * B), 0) == 0, 1.0, 0.0).astype(jnp.bfloat16)

    def step(t, _):
        cg = t // 4
        rg = jnp.where(t < 12, t % 4, 3 - t % 4)
        for k in range(0, 12, 2):
            @pl.when(t == k)
            def _():
                s = k + 4
                wait_col(s)
                if s in pass_on:
                    pass_on[s].start()
                siblings[s].start()

            @pl.when(t == k + 1)
            def _():
                wait_col(k + 5)

        for k in range(4):
            @pl.when(t == k)
            def _():
                for s in range(4 * k, 4 * k + 4):
                    if s:
                        row_copy(plane_back(s)).wait_recv()

        c0, r0 = cg * G, rg * G
        chunk = cols[pl.ds(c0, G)]
        lhs = jnp.concatenate(
            [chunk[:, :B].reshape(G * B, W), colaug[pl.ds(c0, G)].reshape(G * B, W)], axis=1)
        pt = jnp.concatenate(
            [chunk[k, B + h * KC:B + (h + 1) * KC] for k in range(G) for h in range(2)], axis=1)
        pt = jnp.concatenate([pt, ones], axis=0)
        rhs = jnp.concatenate([rows[r0 + k] for k in range(G)], axis=1)
        g = jnp.dot(lhs, rhs, preferred_element_type=jnp.float32)
        a = jnp.exp2(g * coef)
        eye = lax.broadcasted_iota(jnp.int32, (B, B), 0) == lax.broadcasted_iota(jnp.int32, (B, B), 1)
        first = jnp.where(eye & (t == 0), 0.0, a[:B, :B])
        a = jnp.concatenate([jnp.concatenate([first, a[:B, B:]], axis=1), a[B:]], axis=0)
        o = jnp.dot(pt, a.astype(jnp.bfloat16), preferred_element_type=jnp.float32)
        for k in range(G):
            acc[r0 + k] += o[:, k * B:(k + 1) * B]

        augment(jnp.minimum(t + 4, 15))

        for k in range(12, 15):
            @pl.when(t == k)
            def _():
                for s in range(4 * (15 - k), 4 * (15 - k) + 4):
                    red[s].start()
        return 0

    lax.fori_loop(0, 16, step, 0)
    for s in range(1, 4):
        red[s].start()
    sums = acc[0, :KS, :]
    for s in range(15, 0, -1):
        red[plane_back(s)].wait_recv()
        sums = sums + recvp[s]
    walked = sums[:KC, :] / sums[KC:KC + 1, :]

    part = jnp.sum(walked * walked, axis=1, keepdims=True)
    diag = lax.broadcasted_iota(jnp.int32, (KC, 128), 0) == lax.broadcasted_iota(jnp.int32, (KC, 128), 1)
    flat = jnp.sum(jnp.where(diag, part, 0.0), axis=0, keepdims=True)

    def stage(k, flat, where, back, ss, rs):
        st_send[k] = jnp.broadcast_to(flat, (8, 128))
        cps = []
        for s in range(15, 0, -1):
            cp = pltpu.make_async_remote_copy(
                src_ref=st_send.at[k], dst_ref=st_recv.at[k, back(s)],
                send_sem=ss.at[s], recv_sem=rs.at[back(s)],
                device_id=where(s), device_id_type=MESH)
            cp.start()
            cps.append(cp)
        for cp in cps:
            cp.wait_recv()
        for s in range(1, 16):
            flat = flat + st_recv[k, s, 0:1, :]
        return flat, cps

    flat, c1 = stage(0, flat, plane, plane_back, a_s, a_r)
    flat, c2 = stage(1, flat, line, line_back, b_s, b_r)
    mean = jnp.sum(jnp.where(diag, jnp.broadcast_to(flat, (KC, 128)), 0.0), axis=1, keepdims=True) / total
    out_ref[...] = walked / jnp.sqrt(mean + 1e-6)

    for cp in row_sends + col_sends + list(siblings.values()) + list(pass_on.values()) + list(red.values()) + c1 + c2:
        cp.wait_send()


def per_device(total, points, spread, panel):
    dma = pltpu.SemaphoreType.DMA((16,))
    return pl.pallas_call(
        functools.partial(kernel, total),
        out_shape=jax.ShapeDtypeStruct((KC, B), jnp.float32),
        in_specs=[pl.BlockSpec(memory_space=pltpu.SMEM)] + [pl.BlockSpec(memory_space=pltpu.VMEM)] * 2,
        out_specs=pl.BlockSpec(memory_space=pltpu.VMEM),
        scratch_shapes=[
            pltpu.VMEM((16, 2 * W, B), jnp.bfloat16),
            pltpu.VMEM((16, MSG, W), jnp.bfloat16),
            pltpu.VMEM((16, B, W), jnp.bfloat16),
            pltpu.VMEM((16, KR, B), jnp.float32),
            pltpu.VMEM((16, KS, B), jnp.float32),
            pltpu.VMEM((2, 8, 128), jnp.float32),
            pltpu.VMEM((2, 16, 8, 128), jnp.float32),
        ] + [dma] * 12,
        compiler_params=pltpu.CompilerParams(
            collective_id=0, has_side_effects=True, vmem_limit_bytes=48 << 20),
        cost_estimate=pl.CostEstimate(flops=2 * 4096 * 4096 * 160, bytes_accessed=1 << 20, transcendentals=4096 * 4096),
        name="walk",
    )(spread, points, panel.T)


def solution(mesh):
    P = jax.sharding.PartitionSpec
    total = float(B * mesh.size)
    return jax.shard_map(
        functools.partial(per_device, total),
        mesh=mesh,
        in_specs=(P(("rowblk", "colblk"), None), P(), P(("rowblk", "colblk"), None)),
        out_specs=P(None, ("rowblk", "colblk")),
        check_vma=False,
    )
```

time: 117 us -> 64.4 us (0.55)
  Pallas kernels: 114 us -> 61.3 us
    pallas_call x1, Pallas kernels: 114 us -> 61.3 us  [per_device(): pl.pallas_call(functools.partial(kernel, total), out_shape=jax.ShapeDtype...]
where the time goes in v2:
time: 64.4 us; the launch traced here: 64.2 us
  Pallas kernels  61.3 us (95%)
  local copies, waits for them, and re-layouts  2.17 us (3%)
  between operations  0.67 us (1%)
    pallas_call x1, Pallas kernels, per_device(): pl.pallas_call(functools.partial(kernel, total), out_shape=jax.ShapeDtype...  61.3 us
    unnamed x5, local copies, waits for them, and re-layouts  2.17 us

profile of v2, /device:TPU:1, one launch (start us, length us, event | category | flops | bytes accessed | tf_op | source)
XLA Modules:
  0.0 64.2 jit_solution(7753307768025404870)
XLA Ops:
  0.7 0.0 copy-start
  0.7 0.8 %copy-done = bf16[256,128]{1,0:T(8,128)(2,1)S(1)} copy-done((bf16[256,128]{1,0:T(8,128)(2,1)S(1)}, bf16[256,128]{1,0:T(8,128)(2,1)}, u32[]{:S(2)}) %copy-start) | copy-done | bytes 65560
  1.5 0.0 copy-start.1
  1.5 0.7 %copy-done.1 = bf16[256,32]{0,1:T(8,128)(2,1)S(1)} copy-done((bf16[256,32]{0,1:T(8,128)(2,1)S(1)}, bf16[256,32]{0,1:T(8,128)(2,1)}, u32[]{:S(2)}) %copy-start.1) | copy-done | bytes 16408
  2.2 61.3 %walk.1 = f32[32,256]{1,0:T(8,128)S(1)} custom-call(f32[1]{0:T(128)S(6)} %copy.5.spread_ref, bf16[256,128]{1,0:T(8,128)(2,1)S(1)} %copy-done, bf16[32,256]{1,0:T(8,128)(2,1)S(1)} %bitcast.1), custom_call_target="tpu_custom_call" | custom-call | flops 5368709120 | bytes 1048576 | tf_op jit(solution)/shard_map/walk/pallas_call | solution.py:239
  63.6 0.6 copy.6
Async XLA Ops:
  0.7 0.8 %copy-start = (bf16[256,128]{1,0:T(8,128)(2,1)S(1)}, bf16[256,128]{1,0:T(8,128)(2,1)}, u32[]{:S(2)}) copy-start(bf16[256,128]{1,0:T(8,128)(2,1)} %points_ref.1) | copy-start | bytes 196612
  1.5 0.7 %copy-start.1 = (bf16[256,32]{0,1:T(8,128)(2,1)S(1)}, bf16[256,32]{0,1:T(8,128)(2,1)}, u32[]{:S(2)}) copy-start(bf16[256,32]{0,1:T(8,128)(2,1)} %param.5) | copy-start | bytes 49156

commit v3 on v2

--- a/solution.py
+++ b/solution.py
@@ -16,11 +16,12 @@
 KS = 40
 AUG = 16
 G = 4
+HALF = 80
 MSG = B + 2 * KC
 
 PLANE = (
-    (0, 0), (0, 1), (0, 3), (1, 0), (3, 0), (0, 2), (1, 1), (1, 3),
-    (2, 0), (3, 1), (3, 3), (1, 2), (2, 1), (2, 3), (3, 2), (2, 2),
+    (0, 0), (0, 1), (0, 3), (1, 0), (3, 0), (0, 2), (2, 0), (1, 1),
+    (1, 3), (3, 1), (3, 3), (1, 2), (2, 1), (2, 3), (3, 2), (2, 2),
 )
 LINE = tuple((dz, dc) for dz in (0, 1, 7, 2, 6, 3, 5, 4) for dc in (0, 1))
 
@@ -45,7 +46,7 @@
     total,
     spread_ref, points_ref, panel_ref, out_ref,
     rows, cols, colaug, acc, recvp, st_send, st_recv,
-    row_s, row_r, col_s, col_r, sib_s, fwd_s, red_s, red_r, a_s, a_r, b_s, b_r,
+    row_s, row_r, rowa_s, rowa_r, rowb_s, rowb_r, col_s, col_r, sib_s, fwd_s, red_s, red_r, a_s, a_r, b_s, b_r,
 ):
     r = lax.axis_index("rowblk")
     c = lax.axis_index("colblk")
@@ -106,6 +107,30 @@
             src_ref=rows.at[0, pl.ds(0, W + AUG)], dst_ref=rows.at[t, pl.ds(0, W + AUG)],
             send_sem=row_s.at[s], recv_sem=row_r.at[t], device_id=plane(s), device_id_type=MESH)
 
+    def half_copy(src, to, dst, part, ss, rs):
+        return pltpu.make_async_remote_copy(
+            src_ref=rows.at[src, part], dst_ref=rows.at[dst, part],
+            send_sem=ss.at[dst], recv_sem=rs.at[dst], device_id=plane(to), device_id_type=MESH)
+
+    row_pass = {}
+    for e in (1, 3, 2):
+        for d in (1, 3, 2):
+            src, to = PLANE.index((0, d)), PLANE.index((e, 0))
+            row_pass.setdefault(src, []).append(
+                half_copy(src, to, PLANE.index(((4 - e) % 4, d)), pl.ds(0, HALF), rowa_s, rowa_r))
+            src, to = PLANE.index((d, 0)), PLANE.index((0, e))
+            row_pass.setdefault(src, []).append(
+                half_copy(src, to, PLANE.index((d, (4 - e) % 4)), pl.ds(HALF, W + AUG - HALF), rowb_s, rowb_r))
+
+    def row_in(s):
+        row_copy(plane_back(s)).wait_recv()
+        for cp in row_pass[s]:
+            cp.start()
+
+    def halves_in(s):
+        half_copy(0, 1, s, pl.ds(0, HALF), rowa_s, rowa_r).wait_recv()
+        half_copy(0, 1, s, pl.ds(HALF, W + AUG - HALF), rowb_s, rowb_r).wait_recv()
+
     def col_copy(src, dst, sem, where):
         return pltpu.make_async_remote_copy(
             src_ref=cols.at[src], dst_ref=cols.at[dst],
@@ -119,8 +144,8 @@
 
     col_sends = [sibling_copy(0)]
     col_sends += [col_copy(0, line_back(s), col_s.at[s], line(s)) for s in (2, 4, 6, 8)]
-    row_sends = [row_copy(s) for s in range(1, 16)]
-    for cp in col_sends[:3] + row_sends[:3] + col_sends[3:] + row_sends[3:]:
+    row_sends = [row_copy(s) for s in range(1, 7)]
+    for cp in col_sends[:3] + row_sends + col_sends[3:]:
         cp.start()
 
     pass_on = {
@@ -130,14 +155,34 @@
     }
     siblings = {s: sibling_copy(s) for s in range(2, 16, 2)}
 
+    for s in (1, 2, 3, 4):
+        row_in(s)
     wait_col(2)
     siblings[2].start()
+    wait_col(4)
+    siblings[4].start()
     wait_col(1)
     augment(1)
     augment(2)
     wait_col(3)
     augment(3)
 
+    def col_in(s):
+        wait_col(s)
+        if s in pass_on:
+            pass_on[s].start()
+        siblings[s].start()
+
+    events = {
+        0: (lambda: row_in(5), lambda: row_in(6), lambda: col_in(6), lambda: wait_col(5)),
+        1: (lambda: col_in(8), lambda: wait_col(7), lambda: halves_in(7)),
+        2: (lambda: wait_col(9),),
+        3: (lambda: col_in(10),),
+        4: (lambda: col_in(12), lambda: wait_col(11)) + tuple(functools.partial(halves_in, s) for s in range(8, 12)),
+        5: (lambda: col_in(14), lambda: wait_col(13)),
+        6: (lambda: wait_col(15),) + tuple(functools.partial(halves_in, s) for s in range(12, 16)),
+    }
+
     def reduce_copy(s):
         t = plane_back(s)
         return pltpu.make_async_remote_copy(
@@ -148,27 +193,14 @@
     ones = jnp.where(lax.broadcasted_iota(jnp.int32, (KR - KC, G * B), 0) == 0, 1.0, 0.0).astype(jnp.bfloat16)
 
     def step(t, _):
-        cg = t // 4
-        rg = jnp.where(t < 12, t % 4, 3 - t % 4)
-        for k in range(0, 12, 2):
+        early = t < 4
+        cg = jnp.where(t < 8, jnp.where(early, t // 2, t % 2), 2 + t % 2)
+        rg = jnp.where(t < 8, jnp.where(early, t % 2, t // 2), 7 - t // 2)
+        for k, todo in events.items():
             @pl.when(t == k)
             def _():
-                s = k + 4
-                wait_col(s)
-                if s in pass_on:
-                    pass_on[s].start()
-                siblings[s].start()
-
-            @pl.when(t == k + 1)
-            def _():
-                wait_col(k + 5)
-
-        for k in range(4):
-            @pl.when(t == k)
-            def _():
-                for s in range(4 * k, 4 * k + 4):
-                    if s:
-                        row_copy(plane_back(s)).wait_recv()
+                for f in todo:
+                    f()
 
         c0, r0 = cg * G, rg * G
         chunk = cols[pl.ds(c0, G)]
@@ -187,12 +219,14 @@
         for k in range(G):
             acc[r0 + k] += o[:, k * B:(k + 1) * B]
 
-        augment(jnp.minimum(t + 4, 15))
-
-        for k in range(12, 15):
-            @pl.when(t == k)
+        pair = jnp.where(t < 3, 4 + 2 * t, jnp.minimum(2 + 2 * t, 14))
+        augment(pair)
+        augment(pair + 1)
+
+        for k in range(1, 4):
+            @pl.when(t == 15 - 2 * k)
             def _():
-                for s in range(4 * (15 - k), 4 * (15 - k) + 4):
+                for s in range(4 * k, 4 * k + 4):
                     red[s].start()
         return 0
 
@@ -230,7 +264,7 @@
     mean = jnp.sum(jnp.where(diag, jnp.broadcast_to(flat, (KC, 128)), 0.0), axis=1, keepdims=True) / total
     out_ref[...] = walked / jnp.sqrt(mean + 1e-6)
 
-    for cp in row_sends + col_sends + list(siblings.values()) + list(pass_on.values()) + list(red.values()) + c1 + c2:
+    for cp in row_sends + sum(row_pass.values(), []) + col_sends + list(siblings.values()) + list(pass_on.values()) + list(red.values()) + c1 + c2:
         cp.wait_send()
 
 
@@ -249,7 +283,7 @@
             pltpu.VMEM((16, KS, B), jnp.float32),
             pltpu.VMEM((2, 8, 128), jnp.float32),
             pltpu.VMEM((2, 16, 8, 128), jnp.float32),
-        ] + [dma] * 12,
+        ] + [dma] * 16,
         compiler_params=pltpu.CompilerParams(
             collective_id=0, has_side_effects=True, vmem_limit_bytes=48 << 20),
         cost_estimate=pl.CostEstimate(flops=2 * 4096 * 4096 * 160, bytes_accessed=1 << 20, transcendentals=4096 * 4096),

time: 64.4 us -> 57.9 us (0.90)
  Pallas kernels: 61.3 us -> 54.9 us
    pallas_call x1, Pallas kernels: 61.3 us -> 54.9 us  [per_device(): pl.pallas_call(functools.partial(kernel, total), out_shape=jax.ShapeDtype...]
where the time goes in v3:
time: 57.9 us; the launch traced here: 57.7 us
  Pallas kernels  54.9 us (95%)
  local copies, waits for them, and re-layouts  2.17 us (4%)
  between operations  0.67 us (1%)
    pallas_call x1, Pallas kernels, per_device(): pl.pallas_call(functools.partial(kernel, total), out_shape=jax.ShapeDtype...  54.9 us
    unnamed x5, local copies, waits for them, and re-layouts  2.17 us

profile of v3, /device:TPU:1, one launch (start us, length us, event | category | flops | bytes accessed | tf_op | source)
XLA Modules:
  0.0 57.7 jit_solution(768082726829726306)
XLA Ops:
  0.7 0.0 copy-start
  0.7 0.8 %copy-done = bf16[256,128]{1,0:T(8,128)(2,1)S(1)} copy-done((bf16[256,128]{1,0:T(8,128)(2,1)S(1)}, bf16[256,128]{1,0:T(8,128)(2,1)}, u32[]{:S(2)}) %copy-start) | copy-done | bytes 65560
  1.5 0.0 copy-start.1
  1.5 0.7 %copy-done.1 = bf16[256,32]{0,1:T(8,128)(2,1)S(1)} copy-done((bf16[256,32]{0,1:T(8,128)(2,1)S(1)}, bf16[256,32]{0,1:T(8,128)(2,1)}, u32[]{:S(2)}) %copy-start.1) | copy-done | bytes 16408
  2.2 54.9 %walk.1 = f32[32,256]{1,0:T(8,128)S(1)} custom-call(f32[1]{0:T(128)S(6)} %copy.5.spread_ref, bf16[256,128]{1,0:T(8,128)(2,1)S(1)} %copy-done, bf16[32,256]{1,0:T(8,128)(2,1)S(1)} %bitcast.1), custom_call_target="tpu_custom_call" | custom-call | flops 5368709120 | bytes 1048576 | tf_op jit(solution)/shard_map/walk/pallas_call | solution.py:273
  57.1 0.6 %copy.6 = f32[32,256]{1,0:T(8,128)} copy(f32[32,256]{1,0:T(8,128)S(1)} %walk.1) | data formatting | bytes 65536
Async XLA Ops:
  0.7 0.8 %copy-start = (bf16[256,128]{1,0:T(8,128)(2,1)S(1)}, bf16[256,128]{1,0:T(8,128)(2,1)}, u32[]{:S(2)}) copy-start(bf16[256,128]{1,0:T(8,128)(2,1)} %points_ref.1) | copy-start | bytes 196612
  1.5 0.7 %copy-start.1 = (bf16[256,32]{0,1:T(8,128)(2,1)S(1)}, bf16[256,32]{0,1:T(8,128)(2,1)}, u32[]{:S(2)}) copy-start(bf16[256,32]{0,1:T(8,128)(2,1)} %param.5) | copy-start | bytes 49156

commit v4 on v3

--- a/solution.py
+++ b/solution.py
@@ -23,7 +23,12 @@
     (0, 0), (0, 1), (0, 3), (1, 0), (3, 0), (0, 2), (2, 0), (1, 1),
     (1, 3), (3, 1), (3, 3), (1, 2), (2, 1), (2, 3), (3, 2), (2, 2),
 )
-LINE = tuple((dz, dc) for dz in (0, 1, 7, 2, 6, 3, 5, 4) for dc in (0, 1))
+LINE = (
+    (0, 0), (0, 1), (1, 0), (7, 0), (1, 1), (7, 1), (2, 0), (6, 0),
+    (2, 1), (6, 1), (3, 0), (5, 0), (3, 1), (5, 1), (4, 0), (4, 1),
+)
+NEAR_PLANE = (1, 2, 3, 4, 5, 6)
+NEAR_LINE = (1, 2, 3, 6, 7)
 
 
 def plane_back(s):
@@ -45,8 +50,8 @@
 def kernel(
     total,
     spread_ref, points_ref, panel_ref, out_ref,
-    rows, cols, colaug, acc, recvp, st_send, st_recv,
-    row_s, row_r, rowa_s, rowa_r, rowb_s, rowb_r, col_s, col_r, sib_s, fwd_s, red_s, red_r, a_s, a_r, b_s, b_r,
+    rows, cols, panel, colaug, acc, recvp, st_send, st_recv,
+    row_s, row_r, rowa_s, rowa_r, rowb_s, rowb_r, col_s, col_r, sib_s, fwd_s, in_s, red_s, red_r, a_s, a_r, b_s, b_r,
 ):
     r = lax.axis_index("rowblk")
     c = lax.axis_index("colblk")
@@ -66,11 +71,27 @@
         return dev(x, y, (z + dz) % 8, (core + dc) % 2)
 
     barrier = pltpu.get_barrier_semaphore()
-    for s in range(1, 16):
+    for s in NEAR_LINE:
+        pl.semaphore_signal(barrier, inc=1, device_id=line(s), device_id_type=MESH)
+    for s in NEAR_PLANE:
         pl.semaphore_signal(barrier, inc=1, device_id=plane(s), device_id_type=MESH)
-        pl.semaphore_signal(barrier, inc=1, device_id=line(s), device_id_type=MESH)
-
-    pts = points_ref[...]
+
+    fetch = [
+        pltpu.make_async_copy(points_ref, cols.at[0, pl.ds(0, B)], in_s.at[0]),
+        pltpu.make_async_copy(panel_ref, panel, in_s.at[1]),
+    ]
+    for cp in fetch:
+        cp.start()
+
+    def fill(s, _):
+        rows[s, W + AUG:, :] = jnp.zeros((W - AUG, B), jnp.bfloat16)
+        return 0
+    lax.fori_loop(0, 16, fill, 0)
+    acc[...] = jnp.zeros_like(acc)
+    for cp in fetch:
+        cp.wait()
+
+    pts = cols[0, :B, :]
     ptst = pts.astype(jnp.float32).T
     hi, mid, lo = three_terms(-0.5 * jnp.sum(ptst * ptst, axis=0, keepdims=True))
     row = lax.broadcasted_iota(jnp.int32, (AUG, B), 0)
@@ -78,15 +99,8 @@
     aug = jnp.where((row >= 3) & (row < 6), 1.0, aug)
     rows[0, :W, :] = ptst.astype(jnp.bfloat16)
     rows[0, W:W + AUG, :] = aug.astype(jnp.bfloat16)
-    cols[0, :B, :] = pts
-    cols[0, B:B + KC, :] = panel_ref[:, :W]
-    cols[0, B + KC:, :] = panel_ref[:, W:]
-
-    def fill(s, _):
-        rows[s, W + AUG:, :] = jnp.zeros((W - AUG, B), jnp.bfloat16)
-        return 0
-    lax.fori_loop(0, 16, fill, 0)
-    acc[...] = jnp.zeros_like(acc)
+    cols[0, B:B + KC, :] = panel[:, :W]
+    cols[0, B + KC:, :] = panel[:, W:]
 
     coef = LOG2E / (spread_ref[0] * spread_ref[0])
 
@@ -99,7 +113,7 @@
 
     augment(0)
 
-    pl.semaphore_wait(barrier, 30)
+    pl.semaphore_wait(barrier, len(NEAR_LINE) + len(NEAR_PLANE))
 
     def row_copy(s):
         t = plane_back(s)
@@ -131,71 +145,96 @@
         half_copy(0, 1, s, pl.ds(0, HALF), rowa_s, rowa_r).wait_recv()
         half_copy(0, 1, s, pl.ds(HALF, W + AUG - HALF), rowb_s, rowb_r).wait_recv()
 
-    def col_copy(src, dst, sem, where):
+    def col_copy(src, dst, sem, where, part=pl.ds(0, MSG), arrival=None):
         return pltpu.make_async_remote_copy(
-            src_ref=cols.at[src], dst_ref=cols.at[dst],
-            send_sem=sem, recv_sem=col_r.at[dst], device_id=where, device_id_type=MESH)
-
-    def sibling_copy(s):
-        return col_copy(s, s + 1, sib_s.at[s // 2], line(1))
+            src_ref=cols.at[src, part], dst_ref=cols.at[dst, part],
+            send_sem=sem, recv_sem=col_r.at[dst if arrival is None else arrival], device_id=where, device_id_type=MESH)
 
     def wait_col(s):
         col_copy(0, s, sib_s.at[0], line(1)).wait_recv()
 
-    col_sends = [sibling_copy(0)]
-    col_sends += [col_copy(0, line_back(s), col_s.at[s], line(s)) for s in (2, 4, 6, 8)]
-    row_sends = [row_copy(s) for s in range(1, 7)]
-    for cp in col_sends[:3] + row_sends + col_sends[3:]:
+    at = LINE.index
+    half = MSG // 2
+    col_pass = {
+        0: [
+            col_copy(0, at((1, 0)), fwd_s.at[0], line(at((7, 0)))),
+            col_copy(0, at((7, 0)), fwd_s.at[1], line(at((1, 0)))),
+            col_copy(0, at((0, 1)), sib_s.at[0], line(1)),
+            col_copy(0, at((2, 0)), fwd_s.at[2], line(at((6, 0)))),
+            col_copy(0, at((6, 0)), fwd_s.at[3], line(at((2, 0)))),
+        ],
+        at((1, 0)): [], at((7, 0)): [],
+        at((2, 0)): [
+            col_copy(at((2, 0)), at((3, 0)), fwd_s.at[4], line(at((7, 0)))),
+            col_copy(at((2, 0)), at((4, 0)), fwd_s.at[6], line(at((6, 0))), pl.ds(0, half)),
+        ],
+        at((6, 0)): [
+            col_copy(at((6, 0)), at((5, 0)), fwd_s.at[5], line(at((1, 0)))),
+            col_copy(at((6, 0)), at((4, 0)), fwd_s.at[7], line(at((2, 0))), pl.ds(half, half), 16),
+        ],
+        at((3, 0)): [], at((5, 0)): [], at((4, 0)): [],
+    }
+    for dz in range(1, 8):
+        s = at((dz, 0))
+        col_pass[s].append(col_copy(s, at((dz, 1)), sib_s.at[dz], line(1)))
+    row_sends = [row_copy(s) for s in (1, 2, 3, 4, 5, 6)]
+
+    def col_in(s):
+        if LINE[s] == (4, 0):
+            col_pass[at((2, 0))][1].wait_recv()
+            col_pass[at((6, 0))][1].wait_recv()
+        else:
+            wait_col(s)
+        for cp in col_pass[s]:
+            cp.start()
+
+    for cp in col_pass[0][:3] + row_sends[:4] + col_pass[0][3:] + row_sends[4:]:
         cp.start()
 
-    pass_on = {
-        6: col_copy(6, 10, fwd_s.at[0], line(4)),
-        8: col_copy(8, 12, fwd_s.at[1], line(2)),
-        10: col_copy(10, 14, fwd_s.at[2], line(4)),
-    }
-    siblings = {s: sibling_copy(s) for s in range(2, 16, 2)}
-
+    col_in(2)
+    col_in(3)
     for s in (1, 2, 3, 4):
         row_in(s)
-    wait_col(2)
-    siblings[2].start()
-    wait_col(4)
-    siblings[4].start()
     wait_col(1)
-    augment(1)
-    augment(2)
-    wait_col(3)
-    augment(3)
-
-    def col_in(s):
-        wait_col(s)
-        if s in pass_on:
-            pass_on[s].start()
-        siblings[s].start()
-
+    for s in (1, 2, 3):
+        augment(s)
+
+    def pair_augment(s):
+        augment(s)
+        augment(s + 1)
+
+    call = functools.partial
     events = {
-        0: (lambda: row_in(5), lambda: row_in(6), lambda: col_in(6), lambda: wait_col(5)),
-        1: (lambda: col_in(8), lambda: wait_col(7), lambda: halves_in(7)),
-        2: (lambda: wait_col(9),),
-        3: (lambda: col_in(10),),
-        4: (lambda: col_in(12), lambda: wait_col(11)) + tuple(functools.partial(halves_in, s) for s in range(8, 12)),
-        5: (lambda: col_in(14), lambda: wait_col(13)),
-        6: (lambda: wait_col(15),) + tuple(functools.partial(halves_in, s) for s in range(12, 16)),
+        1: (call(row_in, 5), call(row_in, 6), call(wait_col, 4), call(wait_col, 5), call(col_in, 6), call(col_in, 7), call(halves_in, 7)),
+        2: (call(pair_augment, 6),),
+        4: (call(col_in, 10), call(col_in, 11)) + tuple(call(halves_in, s) for s in range(8, 12)),
+        5: (call(wait_col, 8), call(wait_col, 9)),
+        6: tuple(call(halves_in, s) for s in range(12, 16)) + (call(col_in, 14), call(wait_col, 12), call(wait_col, 13)),
+        8: (call(wait_col, 15), ),
     }
+    order = ((0, 0), (0, 1), (1, 0), (1, 1), (0, 2), (1, 2), (0, 3), (1, 3), (2, 3), (3, 3), (2, 2), (3, 2), (2, 1), (3, 1), (2, 0), (3, 0))
+    complete = {9: 3, 11: 2, 13: 1}
+    pairs = {1: 4, 4: 10, 5: 8, 6: 12, 8: 14}
+
+    def choose(t, table):
+        out = jnp.int32(0)
+        for k, v in table.items():
+            if v:
+                out = jnp.where(t == k, v, out)
+        return out
 
     def reduce_copy(s):
         t = plane_back(s)
         return pltpu.make_async_remote_copy(
-            src_ref=acc.at[s, pl.ds(0, KS)], dst_ref=recvp.at[t],
+            src_ref=acc.at[s, pl.ds(0, KS)], dst_ref=recvp.at[t, pl.ds(0, KS)],
             send_sem=red_s.at[s], recv_sem=red_r.at[t], device_id=plane(s), device_id_type=MESH)
 
     red = {s: reduce_copy(s) for s in range(1, 16)}
     ones = jnp.where(lax.broadcasted_iota(jnp.int32, (KR - KC, G * B), 0) == 0, 1.0, 0.0).astype(jnp.bfloat16)
 
     def step(t, _):
-        early = t < 4
-        cg = jnp.where(t < 8, jnp.where(early, t // 2, t % 2), 2 + t % 2)
-        rg = jnp.where(t < 8, jnp.where(early, t % 2, t // 2), 7 - t // 2)
+        cg = choose(t, {k: v[0] for k, v in enumerate(order)})
+        rg = choose(t, {k: v[1] for k, v in enumerate(order)})
         for k, todo in events.items():
             @pl.when(t == k)
             def _():
@@ -219,14 +258,14 @@
         for k in range(G):
             acc[r0 + k] += o[:, k * B:(k + 1) * B]
 
-        pair = jnp.where(t < 3, 4 + 2 * t, jnp.minimum(2 + 2 * t, 14))
+        pair = choose(t, pairs)
         augment(pair)
         augment(pair + 1)
 
-        for k in range(1, 4):
-            @pl.when(t == 15 - 2 * k)
+        for k, q in complete.items():
+            @pl.when(t == k)
             def _():
-                for s in range(4 * k, 4 * k + 4):
+                for s in range(4 * q, 4 * q + 4):
                     red[s].start()
         return 0
 
@@ -236,7 +275,7 @@
     sums = acc[0, :KS, :]
     for s in range(15, 0, -1):
         red[plane_back(s)].wait_recv()
-        sums = sums + recvp[s]
+        sums = sums + recvp[s, :KS]
     walked = sums[:KC, :] / sums[KC:KC + 1, :]
 
     part = jnp.sum(walked * walked, axis=1, keepdims=True)
@@ -264,26 +303,27 @@
     mean = jnp.sum(jnp.where(diag, jnp.broadcast_to(flat, (KC, 128)), 0.0), axis=1, keepdims=True) / total
     out_ref[...] = walked / jnp.sqrt(mean + 1e-6)
 
-    for cp in row_sends + sum(row_pass.values(), []) + col_sends + list(siblings.values()) + list(pass_on.values()) + list(red.values()) + c1 + c2:
+    for cp in row_sends + sum(row_pass.values(), []) + sum(col_pass.values(), []) + list(red.values()) + c1 + c2:
         cp.wait_send()
 
 
 def per_device(total, points, spread, panel):
-    dma = pltpu.SemaphoreType.DMA((16,))
+    dma = pltpu.SemaphoreType.DMA((24,))
     return pl.pallas_call(
         functools.partial(kernel, total),
         out_shape=jax.ShapeDtypeStruct((KC, B), jnp.float32),
-        in_specs=[pl.BlockSpec(memory_space=pltpu.SMEM)] + [pl.BlockSpec(memory_space=pltpu.VMEM)] * 2,
+        in_specs=[pl.BlockSpec(memory_space=pltpu.SMEM)] + [pl.BlockSpec(memory_space=pltpu.HBM)] * 2,
         out_specs=pl.BlockSpec(memory_space=pltpu.VMEM),
         scratch_shapes=[
             pltpu.VMEM((16, 2 * W, B), jnp.bfloat16),
             pltpu.VMEM((16, MSG, W), jnp.bfloat16),
+            pltpu.VMEM((KC, B), jnp.bfloat16),
             pltpu.VMEM((16, B, W), jnp.bfloat16),
             pltpu.VMEM((16, KR, B), jnp.float32),
-            pltpu.VMEM((16, KS, B), jnp.float32),
+            pltpu.VMEM((16, KR, B), jnp.float32),
             pltpu.VMEM((2, 8, 128), jnp.float32),
             pltpu.VMEM((2, 16, 8, 128), jnp.float32),
-        ] + [dma] * 16,
+        ] + [dma] * 17,
         compiler_params=pltpu.CompilerParams(
             collective_id=0, has_side_effects=True, vmem_limit_bytes=48 << 20),
         cost_estimate=pl.CostEstimate(flops=2 * 4096 * 4096 * 160, bytes_accessed=1 << 20, transcendentals=4096 * 4096),

time: 57.9 us -> 55.8 us (0.964)
  Pallas kernels: 54.9 us -> 52.7 us
    pallas_call x1, Pallas kernels: 54.9 us -> 52.7 us  [per_device(): pl.pallas_call(functools.partial(kernel, total), out_shape=jax.ShapeDtype...]
where the time goes in v4:
time: 55.8 us; the launch traced here: 55.6 us
  Pallas kernels  52.7 us (94%)
  local copies, waits for them, and re-layouts  2.17 us (4%)
  between operations  0.67 us (1%)
    pallas_call x1, Pallas kernels, per_device(): pl.pallas_call(functools.partial(kernel, total), out_shape=jax.ShapeDtype...  52.7 us
    unnamed x5, local copies, waits for them, and re-layouts  2.17 us

profile of v4, /device:TPU:1, one launch (start us, length us, event | category | flops | bytes accessed | tf_op | source)
XLA Modules:
  0.0 55.6 jit_solution(72022633368847002)
XLA Ops:
  0.7 0.0 copy-start
  0.7 0.8 %copy-done = bf16[256,128]{1,0:T(8,128)(2,1)S(1)} copy-done((bf16[256,128]{1,0:T(8,128)(2,1)S(1)}, bf16[256,128]{1,0:T(8,128)(2,1)}, u32[]{:S(2)}) %copy-start) | copy-done | bytes 65560
  1.5 0.0 copy-start.1
  1.5 0.7 %copy-done.1 = bf16[256,32]{0,1:T(8,128)(2,1)S(1)} copy-done((bf16[256,32]{0,1:T(8,128)(2,1)S(1)}, bf16[256,32]{0,1:T(8,128)(2,1)}, u32[]{:S(2)}) %copy-start.1) | copy-done | bytes 16408
  2.2 52.7 %walk.1 = f32[32,256]{1,0:T(8,128)S(1)} custom-call(f32[1]{0:T(128)S(6)} %copy.5.spread_ref, bf16[256,128]{1,0:T(8,128)(2,1)S(1)} %copy-done, bf16[32,256]{1,0:T(8,128)(2,1)S(1)} %bitcast.1), custom_call_target="tpu_custom_call" | custom-call | flops 5368709120 | bytes 1048576 | tf_op jit(solution)/shard_map/walk/pallas_call | solution.py:312
  55.0 0.6 %copy.6 = f32[32,256]{1,0:T(8,128)} copy(f32[32,256]{1,0:T(8,128)S(1)} %walk.1) | data formatting | bytes 65536
Async XLA Ops:
  0.7 0.8 %copy-start = (bf16[256,128]{1,0:T(8,128)(2,1)S(1)}, bf16[256,128]{1,0:T(8,128)(2,1)}, u32[]{:S(2)}) copy-start(bf16[256,128]{1,0:T(8,128)(2,1)} %points_ref.1) | copy-start | bytes 196612
  1.5 0.7 %copy-start.1 = (bf16[256,32]{0,1:T(8,128)(2,1)S(1)}, bf16[256,32]{0,1:T(8,128)(2,1)}, u32[]{:S(2)}) copy-start(bf16[256,32]{0,1:T(8,128)(2,1)} %param.5) | copy-start | bytes 49156

commit v5 on v4

--- a/solution.py
+++ b/solution.py
@@ -199,22 +199,52 @@
     for s in (1, 2, 3):
         augment(s)
 
-    def pair_augment(s):
-        augment(s)
-        augment(s + 1)
+    ones = jnp.where(lax.broadcasted_iota(jnp.int32, (KR - KC, 8 * B), 0) == 0, 1.0, 0.0).astype(jnp.bfloat16)
+
+    def chunk(c0, nc, r0, nr, own=False):
+        part = cols[pl.ds(c0, nc)]
+        lhs = jnp.concatenate(
+            [part[:, :B].reshape(nc * B, W), colaug[pl.ds(c0, nc)].reshape(nc * B, W)], axis=1)
+        pt = jnp.concatenate(
+            [part[k, B + h * KC:B + (h + 1) * KC] for k in range(nc) for h in range(2)], axis=1)
+        pt = jnp.concatenate([pt, ones[:, :nc * B]], axis=0)
+        rhs = jnp.concatenate([rows[r0 + k] for k in range(nr)], axis=1)
+        g = jnp.dot(lhs, rhs, preferred_element_type=jnp.float32)
+        a = jnp.exp2(g * coef)
+        if own:
+            eye = lax.broadcasted_iota(jnp.int32, (B, B), 0) == lax.broadcasted_iota(jnp.int32, (B, B), 1)
+            first = jnp.where(eye, 0.0, a[:B, :B])
+            a = jnp.concatenate([jnp.concatenate([first, a[:B, B:]], axis=1), a[B:]], axis=0)
+        o = jnp.dot(pt, a.astype(jnp.bfloat16), preferred_element_type=jnp.float32)
+        for k in range(nr):
+            acc[r0 + k] += o[:, k * B:(k + 1) * B]
+
+    chunk(0, 4, 0, 4, own=True)
+    row_in(5)
+    row_in(6)
+    chunk(0, 4, 4, 3)
+    wait_col(4)
+    wait_col(5)
+    augment(4)
+    augment(5)
+    chunk(4, 2, 0, 7)
+    col_in(6)
+    col_in(7)
+    augment(6)
+    augment(7)
+    chunk(6, 2, 0, 7)
+    halves_in(7)
+    chunk(0, 8, 7, 1)
 
     call = functools.partial
     events = {
-        1: (call(row_in, 5), call(row_in, 6), call(wait_col, 4), call(wait_col, 5), call(col_in, 6), call(col_in, 7), call(halves_in, 7)),
-        2: (call(pair_augment, 6),),
-        4: (call(col_in, 10), call(col_in, 11)) + tuple(call(halves_in, s) for s in range(8, 12)),
-        5: (call(wait_col, 8), call(wait_col, 9)),
-        6: tuple(call(halves_in, s) for s in range(12, 16)) + (call(col_in, 14), call(wait_col, 12), call(wait_col, 13)),
-        8: (call(wait_col, 15), ),
+        0: tuple(call(halves_in, s) for s in range(8, 12)),
+        1: (call(col_in, 10), call(col_in, 11), call(wait_col, 8), call(wait_col, 9)) + tuple(call(halves_in, s) for s in range(12, 16)),
+        2: (call(col_in, 14), call(wait_col, 12), call(wait_col, 13), call(augment, 12), call(augment, 13), call(augment, 14),
+            call(wait_col, 15), call(augment, 15)),
     }
-    order = ((0, 0), (0, 1), (1, 0), (1, 1), (0, 2), (1, 2), (0, 3), (1, 3), (2, 3), (3, 3), (2, 2), (3, 2), (2, 1), (3, 1), (2, 0), (3, 0))
-    complete = {9: 3, 11: 2, 13: 1}
-    pairs = {1: 4, 4: 10, 5: 8, 6: 12, 8: 14}
+    order = ((0, 2), (0, 3), (8, 3), (8, 2), (8, 1), (8, 0))
+    complete = {2: 3, 3: 2, 4: 1}
 
     def choose(t, table):
         out = jnp.int32(0)
@@ -230,37 +260,18 @@
             send_sem=red_s.at[s], recv_sem=red_r.at[t], device_id=plane(s), device_id_type=MESH)
 
     red = {s: reduce_copy(s) for s in range(1, 16)}
-    ones = jnp.where(lax.broadcasted_iota(jnp.int32, (KR - KC, G * B), 0) == 0, 1.0, 0.0).astype(jnp.bfloat16)
-
     def step(t, _):
-        cg = choose(t, {k: v[0] for k, v in enumerate(order)})
-        rg = choose(t, {k: v[1] for k, v in enumerate(order)})
+        c0 = choose(t, {k: v[0] for k, v in enumerate(order)})
+        r0 = G * choose(t, {k: v[1] for k, v in enumerate(order)})
         for k, todo in events.items():
             @pl.when(t == k)
             def _():
                 for f in todo:
                     f()
 
-        c0, r0 = cg * G, rg * G
-        chunk = cols[pl.ds(c0, G)]
-        lhs = jnp.concatenate(
-            [chunk[:, :B].reshape(G * B, W), colaug[pl.ds(c0, G)].reshape(G * B, W)], axis=1)
-        pt = jnp.concatenate(
-            [chunk[k, B + h * KC:B + (h + 1) * KC] for k in range(G) for h in range(2)], axis=1)
-        pt = jnp.concatenate([pt, ones], axis=0)
-        rhs = jnp.concatenate([rows[r0 + k] for k in range(G)], axis=1)
-        g = jnp.dot(lhs, rhs, preferred_element_type=jnp.float32)
-        a = jnp.exp2(g * coef)
-        eye = lax.broadcasted_iota(jnp.int32, (B, B), 0) == lax.broadcasted_iota(jnp.int32, (B, B), 1)
-        first = jnp.where(eye & (t == 0), 0.0, a[:B, :B])
-        a = jnp.concatenate([jnp.concatenate([first, a[:B, B:]], axis=1), a[B:]], axis=0)
-        o = jnp.dot(pt, a.astype(jnp.bfloat16), preferred_element_type=jnp.float32)
-        for k in range(G):
-            acc[r0 + k] += o[:, k * B:(k + 1) * B]
-
-        pair = choose(t, pairs)
-        augment(pair)
-        augment(pair + 1)
+        chunk(c0, 8, r0, G)
+        for k in range(4):
+            augment(jnp.where(t == 0, 0, 8) + k)
 
         for k, q in complete.items():
             @pl.when(t == k)
@@ -269,9 +280,11 @@
                     red[s].start()
         return 0
 
-    lax.fori_loop(0, 16, step, 0)
+    lax.fori_loop(0, 6, step, 0)
     for s in range(1, 4):
         red[s].start()
+    for cp in row_sends + sum(row_pass.values(), []) + sum(col_pass.values(), []):
+        cp.wait_send()
     sums = acc[0, :KS, :]
     for s in range(15, 0, -1):
         red[plane_back(s)].wait_recv()
@@ -282,7 +295,7 @@
     diag = lax.broadcasted_iota(jnp.int32, (KC, 128), 0) == lax.broadcasted_iota(jnp.int32, (KC, 128), 1)
     flat = jnp.sum(jnp.where(diag, part, 0.0), axis=0, keepdims=True)
 
-    def stage(k, flat, where, back, ss, rs):
+    def stage(k, flat, where, back, ss, rs, before):
         st_send[k] = jnp.broadcast_to(flat, (8, 128))
         cps = []
         for s in range(15, 0, -1):
@@ -292,18 +305,20 @@
                 device_id=where(s), device_id_type=MESH)
             cp.start()
             cps.append(cp)
+        for cp in before:
+            cp.wait_send()
         for cp in cps:
             cp.wait_recv()
         for s in range(1, 16):
             flat = flat + st_recv[k, s, 0:1, :]
         return flat, cps
 
-    flat, c1 = stage(0, flat, plane, plane_back, a_s, a_r)
-    flat, c2 = stage(1, flat, line, line_back, b_s, b_r)
+    flat, c1 = stage(0, flat, plane, plane_back, a_s, a_r, list(red.values()))
+    flat, c2 = stage(1, flat, line, line_back, b_s, b_r, c1)
     mean = jnp.sum(jnp.where(diag, jnp.broadcast_to(flat, (KC, 128)), 0.0), axis=1, keepdims=True) / total
     out_ref[...] = walked / jnp.sqrt(mean + 1e-6)
 
-    for cp in row_sends + sum(row_pass.values(), []) + sum(col_pass.values(), []) + list(red.values()) + c1 + c2:
+    for cp in c2:
         cp.wait_send()
 
 
@@ -328,7 +343,7 @@
             collective_id=0, has_side_effects=True, vmem_limit_bytes=48 << 20),
         cost_estimate=pl.CostEstimate(flops=2 * 4096 * 4096 * 160, bytes_accessed=1 << 20, transcendentals=4096 * 4096),
         name="walk",
-    )(spread, points, panel.T)
+    )(spread, pltpu.with_memory_space_constraint(points, pltpu.HBM), pltpu.with_memory_space_constraint(panel.T, pltpu.HBM))
 
 
 def solution(mesh):

time: 55.8 us -> 53.5 us (0.959)
  local copies, waits for them, and re-layouts: 2.17 us -> 0.62 us
  Pallas kernels: 52.7 us -> 52.1 us
    unnamed x5 -> x1, local copies, waits for them, and re-layouts: 2.17 us -> 0.62 us
    pallas_call x1, Pallas kernels: 52.7 us -> 52.1 us  [per_device(): pl.pallas_call(functools.partial(kernel, total), out_shape=jax.ShapeDtype...]
where the time goes in v5:
time: 53.5 us; the launch traced here: 53.4 us
  Pallas kernels  52.1 us (97%)
  between operations  0.66 us (1%)
  local copies, waits for them, and re-layouts  0.62 us (1%)
    pallas_call x1, Pallas kernels, per_device(): pl.pallas_call(functools.partial(kernel, total), out_shape=jax.ShapeDtype...  52.1 us

profile of v5, /device:TPU:1, one launch (start us, length us, event | category | flops | bytes accessed | tf_op | source)
XLA Modules:
  0.0 53.4 jit_solution(11704127383070813828)
XLA Ops:
  0.7 52.1 %walk.1 = f32[32,256]{1,0:T(8,128)S(1)} custom-call(f32[1]{0:T(128)S(6)} %copy.5.spread_ref, bf16[256,128]{1,0:T(8,128)(2,1)} %points_ref.1, bf16[32,256]{1,0:T(8,128)(2,1)} %bitcast.1), custom_call_target="tpu_custom_call" | custom-call | flops 5368709120 | bytes 1048576 | tf_op jit(solution)/shard_map/walk/pallas_call | solution.py:327
  52.8 0.6 %copy.6 = f32[32,256]{1,0:T(8,128)} copy(f32[32,256]{1,0:T(8,128)S(1)} %walk.1) | data formatting | bytes 65536

commit v6 on v5

--- a/solution.py
+++ b/solution.py
@@ -13,7 +13,8 @@
 W = 128
 KC = 32
 KR = 48
-KS = 40
+L = 128
+KS = 2 * KC + 8
 AUG = 16
 G = 4
 HALF = 80
@@ -199,7 +200,9 @@
     for s in (1, 2, 3):
         augment(s)
 
-    ones = jnp.where(lax.broadcasted_iota(jnp.int32, (KR - KC, 8 * B), 0) == 0, 1.0, 0.0).astype(jnp.bfloat16)
+    ones = jnp.where(lax.broadcasted_iota(jnp.int32, (KR - KC, 16 * B), 0) < 2, 1.0, 0.0).astype(jnp.bfloat16)
+
+    upper = lax.broadcasted_iota(jnp.int32, (8, L), 0) == 0
 
     def chunk(c0, nc, r0, nr, own=False):
         part = cols[pl.ds(c0, nc)]
@@ -213,85 +216,81 @@
         a = jnp.exp2(g * coef)
         if own:
             eye = lax.broadcasted_iota(jnp.int32, (B, B), 0) == lax.broadcasted_iota(jnp.int32, (B, B), 1)
-            first = jnp.where(eye, 0.0, a[:B, :B])
-            a = jnp.concatenate([jnp.concatenate([first, a[:B, B:]], axis=1), a[B:]], axis=0)
+            first = jnp.where(eye, 0.0, a[:B])
+            a = jnp.concatenate([first, a[B:]], axis=0)
         o = jnp.dot(pt, a.astype(jnp.bfloat16), preferred_element_type=jnp.float32)
         for k in range(nr):
-            acc[r0 + k] += o[:, k * B:(k + 1) * B]
-
-    chunk(0, 4, 0, 4, own=True)
+            left, right = o[:, k * B:k * B + L], o[:, k * B + L:(k + 1) * B]
+            acc[r0 + k, :KC] += left[:KC]
+            acc[r0 + k, KC:2 * KC] += right[:KC]
+            acc[r0 + k, 2 * KC:] += jnp.where(upper, left[KC:KC + 8], right[KC:KC + 8])
+
+    chunk(0, 4, 1, 4)
     row_in(5)
     row_in(6)
-    chunk(0, 4, 4, 3)
+    chunk(0, 4, 5, 2)
     wait_col(4)
     wait_col(5)
     augment(4)
     augment(5)
-    chunk(4, 2, 0, 7)
+    chunk(4, 2, 1, 6)
     col_in(6)
     col_in(7)
     augment(6)
     augment(7)
-    chunk(6, 2, 0, 7)
-    halves_in(7)
-    chunk(0, 8, 7, 1)
-
-    call = functools.partial
-    events = {
-        0: tuple(call(halves_in, s) for s in range(8, 12)),
-        1: (call(col_in, 10), call(col_in, 11), call(wait_col, 8), call(wait_col, 9)) + tuple(call(halves_in, s) for s in range(12, 16)),
-        2: (call(col_in, 14), call(wait_col, 12), call(wait_col, 13), call(augment, 12), call(augment, 13), call(augment, 14),
-            call(wait_col, 15), call(augment, 15)),
-    }
-    order = ((0, 2), (0, 3), (8, 3), (8, 2), (8, 1), (8, 0))
-    complete = {2: 3, 3: 2, 4: 1}
-
-    def choose(t, table):
-        out = jnp.int32(0)
-        for k, v in table.items():
-            if v:
-                out = jnp.where(t == k, v, out)
-        return out
-
+    chunk(6, 2, 1, 6)
     def reduce_copy(s):
         t = plane_back(s)
         return pltpu.make_async_remote_copy(
-            src_ref=acc.at[s, pl.ds(0, KS)], dst_ref=recvp.at[t, pl.ds(0, KS)],
+            src_ref=acc.at[s], dst_ref=recvp.at[t],
             send_sem=red_s.at[s], recv_sem=red_r.at[t], device_id=plane(s), device_id_type=MESH)
 
     red = {s: reduce_copy(s) for s in range(1, 16)}
-    def step(t, _):
-        c0 = choose(t, {k: v[0] for k, v in enumerate(order)})
-        r0 = G * choose(t, {k: v[1] for k, v in enumerate(order)})
-        for k, todo in events.items():
-            @pl.when(t == k)
-            def _():
-                for f in todo:
-                    f()
-
-        chunk(c0, 8, r0, G)
-        for k in range(4):
-            augment(jnp.where(t == 0, 0, 8) + k)
-
-        for k, q in complete.items():
-            @pl.when(t == k)
-            def _():
-                for s in range(4 * q, 4 * q + 4):
-                    red[s].start()
-        return 0
-
-    lax.fori_loop(0, 6, step, 0)
-    for s in range(1, 4):
-        red[s].start()
+
+    def send_sums(slots):
+        for s in slots:
+            red[s].start()
+
+    for s in range(8, 12):
+        halves_in(s)
+    chunk(0, 8, 8, 4)
+    col_in(10)
+    col_in(11)
+    for s in range(12, 16):
+        halves_in(s)
+    wait_col(8)
+    wait_col(9)
+    for s in range(8, 12):
+        augment(s)
+    chunk(0, 8, 12, 4)
+    col_in(14)
+    wait_col(12)
+    wait_col(13)
+    for s in range(12, 15):
+        augment(s)
+    chunk(8, 4, 12, 4)
+    wait_col(15)
+    augment(15)
+    chunk(12, 4, 12, 4)
+    send_sums(range(12, 16))
+    chunk(8, 8, 8, 4)
+    send_sums(range(8, 12))
+    halves_in(7)
+    chunk(0, 8, 7, 1)
+    chunk(8, 8, 4, 4)
+    send_sums(range(4, 8))
+    chunk(8, 8, 1, 3)
+    send_sums(range(1, 4))
+    chunk(0, 16, 0, 1, own=True)
     for cp in row_sends + sum(row_pass.values(), []) + sum(col_pass.values(), []):
         cp.wait_send()
-    sums = acc[0, :KS, :]
+    sums = acc[0]
     for s in range(15, 0, -1):
         red[plane_back(s)].wait_recv()
-        sums = sums + recvp[s, :KS]
-    walked = sums[:KC, :] / sums[KC:KC + 1, :]
-
-    part = jnp.sum(walked * walked, axis=1, keepdims=True)
+        sums = sums + recvp[s]
+    walked = [sums[h * KC:(h + 1) * KC] / sums[2 * KC + h:2 * KC + h + 1] for h in range(2)]
+
+    part = jnp.sum(walked[0] * walked[0] + walked[1] * walked[1], axis=1, keepdims=True)
     diag = lax.broadcasted_iota(jnp.int32, (KC, 128), 0) == lax.broadcasted_iota(jnp.int32, (KC, 128), 1)
     flat = jnp.sum(jnp.where(diag, part, 0.0), axis=0, keepdims=True)
 
@@ -316,7 +315,9 @@
     flat, c1 = stage(0, flat, plane, plane_back, a_s, a_r, list(red.values()))
     flat, c2 = stage(1, flat, line, line_back, b_s, b_r, c1)
     mean = jnp.sum(jnp.where(diag, jnp.broadcast_to(flat, (KC, 128)), 0.0), axis=1, keepdims=True) / total
-    out_ref[...] = walked / jnp.sqrt(mean + 1e-6)
+    scale = jnp.sqrt(mean + 1e-6)
+    for h in range(2):
+        out_ref[:, h * L:(h + 1) * L] = walked[h] / scale
 
     for cp in c2:
         cp.wait_send()
@@ -334,8 +335,8 @@
             pltpu.VMEM((16, MSG, W), jnp.bfloat16),
             pltpu.VMEM((KC, B), jnp.bfloat16),
             pltpu.VMEM((16, B, W), jnp.bfloat16),
-            pltpu.VMEM((16, KR, B), jnp.float32),
-            pltpu.VMEM((16, KR, B), jnp.float32),
+            pltpu.VMEM((16, KS, L), jnp.float32),
+            pltpu.VMEM((16, KS, L), jnp.float32),
             pltpu.VMEM((2, 8, 128), jnp.float32),
             pltpu.VMEM((2, 16, 8, 128), jnp.float32),
         ] + [dma] * 17,

time: 53.5 us -> 52.1 us (0.974)
  Pallas kernels: 52.1 us -> 50.7 us
    pallas_call x1, Pallas kernels: 52.1 us -> 50.7 us  [per_device(): pl.pallas_call(functools.partial(kernel, total), out_shape=jax.ShapeDtype...]
where the time goes in v6:
time: 52.1 us; the launch traced here: 52 us
  Pallas kernels  50.7 us (97%)
  between operations  0.66 us (1%)
  local copies, waits for them, and re-layouts  0.62 us (1%)
    pallas_call x1, Pallas kernels, per_device(): pl.pallas_call(functools.partial(kernel, total), out_shape=jax.ShapeDtype...  50.7 us

profile of v6, /device:TPU:1, one launch (start us, length us, event | category | flops | bytes accessed | tf_op | source)
XLA Modules:
  0.0 52.0 jit_solution(5100901546897901083)
XLA Ops:
  0.7 50.7 %walk.1 = f32[32,256]{1,0:T(8,128)S(1)} custom-call(f32[1]{0:T(128)S(6)} %copy.5.spread_ref, bf16[256,128]{1,0:T(8,128)(2,1)} %points_ref.1, bf16[32,256]{1,0:T(8,128)(2,1)} %bitcast.1), custom_call_target="tpu_custom_call" | custom-call | flops 5368709120 | bytes 1048576 | tf_op jit(solution)/shard_map/walk/pallas_call | solution.py:328
  51.4 0.6 %copy.6 = f32[32,256]{1,0:T(8,128)} copy(f32[32,256]{1,0:T(8,128)S(1)} %walk.1) | data formatting | bytes 65536

commit v7 on v6

--- a/solution.py
+++ b/solution.py
@@ -253,7 +253,8 @@
 
     for s in range(8, 12):
         halves_in(s)
-    chunk(0, 8, 8, 4)
+    chunk(0, 4, 8, 4)
+    chunk(4, 4, 8, 4)
     col_in(10)
     col_in(11)
     for s in range(12, 16):
@@ -262,8 +263,9 @@
     wait_col(9)
     for s in range(8, 12):
         augment(s)
-    chunk(0, 8, 12, 4)
+    chunk(0, 4, 12, 4)
     col_in(14)
+    chunk(4, 4, 12, 4)
     wait_col(12)
     wait_col(13)
     for s in range(12, 15):

time: 52.1 us -> 51.8 us (level)
  no operation moved by 1% of the time
where the time goes in v7:
time: 51.8 us; the launch traced here: 51.7 us
  Pallas kernels  50.4 us (97%)
  between operations  0.66 us (1%)
  local copies, waits for them, and re-layouts  0.62 us (1%)
    pallas_call x1, Pallas kernels, per_device(): pl.pallas_call(functools.partial(kernel, total), out_shape=jax.ShapeDtype...  50.4 us

profile of v7, /device:TPU:1, one launch (start us, length us, event | category | flops | bytes accessed | tf_op | source)
XLA Modules:
  0.0 51.7 jit_solution(10075426937298722602)
XLA Ops:
  0.7 50.4 %walk.1 = f32[32,256]{1,0:T(8,128)S(1)} custom-call(f32[1]{0:T(128)S(6)} %copy.5.spread_ref, bf16[256,128]{1,0:T(8,128)(2,1)} %points_ref.1, bf16[32,256]{1,0:T(8,128)(2,1)} %bitcast.1), custom_call_target="tpu_custom_call" | custom-call | flops 5368709120 | bytes 1048576 | tf_op jit(solution)/shard_map/walk/pallas_call | solution.py:330
  51.1 0.6 %copy.6 = f32[32,256]{1,0:T(8,128)} copy(f32[32,256]{1,0:T(8,128)S(1)} %walk.1) | data formatting | bytes 65536
